TPU v7x, 32 devices: a whole 2x2x4 slice. The times are simulated.
32 devices in a mesh: ctx: 4 (over x, core), head: 8 (over z, y).
Axes of the slice: x: 2, y: 2, z: 4, core: 2. Of those that a mesh axis runs over, the one named last changes fastest.
Arguments:
- q_latent: bfloat16 [512, 128, 576], P(('ctx', 'head')), may hold values from -84 to 84
- index_query: bfloat16 [512, 64, 128], P('head'), may hold values from -6 to 6
- index_weight: float32 [512, 64], P('head'), may hold values from -0.75 to 0.75
- index_keys: bfloat16 [8192, 128], P('ctx'), may hold values from -6 to 6
- latent_cache: bfloat16 [8192, 576], P('ctx'), may hold values from -6 to 6
- block_ids: int32 [4, 32], replicated, may hold values from 0 to 127, as said below
- block_counts: int32 [4], replicated, may hold values from 24 to 32, as said below
Outputs:
- attention: bfloat16 [512, 128, 512], P('ctx', 'head')
- index_scores: float32 [512, 8192], P('head', 'ctx')
Inputs may be any that keep to these rules, and one draw needn't show every extreme that they name: `block_ids`: row t is query tile t's list of blocks of 64 positions. Its first block_counts[t] entries are distinct, lie at or before the tile's own last block and include the 2 blocks that hold the tile's own queries; of these counted entries at most 8 lie in one context shard of 32 blocks, and exactly 8 lie in the shard of the newest positions. Entries after the count are arbitrary block ids. `block_counts`: some tile has all 32 entries counted.
All inputs are finite; a program needn't handle non-finite values.
Results may differ from a plain program's by a relative error of at most 0.0034.
Values may be sent and summed in bfloat16 or wider, within the bound.
A program may use at most 128 MiB of HBM per device.

v0:
```python
import jax
import jax.numpy as jnp
from jax import lax
from jax.sharding import PartitionSpec as P

ROPE = 64
BLOCK = 64
TILE = 128
CAP = 8


softmax_scale = 192.0 ** (-0.5)


def index_block(index_query, index_weight, key_block):
    flat_query = index_query.reshape(-1, index_query.shape[2])
    raw_dots = lax.dot_general(
        flat_query, key_block, (((1,), (1,)), ((), ())), preferred_element_type=jnp.float32
    )
    gated_dots = jax.nn.relu(raw_dots * index_query.shape[2] ** (-0.5)).reshape(
        index_query.shape[0], index_query.shape[1], -1
    )
    return jnp.sum(gated_dots * index_weight[:, :, None], axis=1)


def attend_rows(query_block, key_rows, allowed, latent_width):
    rows_here = query_block.shape[0]
    heads_here = query_block.shape[1]
    flat_query = query_block.reshape(rows_here * heads_here, -1)
    raw_scores = lax.dot_general(
        flat_query, key_rows, (((1,), (1,)), ((), ())), preferred_element_type=jnp.float32
    )
    raw_scores = raw_scores.reshape(rows_here, heads_here, -1) * softmax_scale
    masked = jnp.where(allowed[:, None, :], raw_scores, -jnp.inf)
    row_max = jnp.max(masked, axis=2, keepdims=True)
    exp_scores = jnp.exp(masked - row_max)
    totals = jnp.sum(exp_scores, axis=2, keepdims=True)
    weights = exp_scores.astype(jnp.bfloat16).reshape(rows_here * heads_here, -1)
    full_sum = jnp.dot(weights, key_rows, preferred_element_type=jnp.float32)
    weighted_sum = full_sum.reshape(rows_here, heads_here, -1)[:, :, :latent_width]
    return (weighted_sum / totals).astype(jnp.bfloat16)


def slot_tables(block_ids, block_counts, blocks_dev, shards, capacity):
    entry_index = jnp.arange(block_ids.shape[1], dtype=jnp.int32)
    is_valid = entry_index[None, :] < block_counts[:, None]
    shard_of = block_ids // blocks_dev
    local_of = block_ids - shard_of * blocks_dev
    earlier = (
        (shard_of[:, :, None] == shard_of[:, None, :])
        & is_valid[:, None, :]
        & (entry_index[None, None, :] < entry_index[None, :, None])
    )
    rank_of = jnp.sum(earlier.astype(jnp.int32), axis=2)
    shard_hit = (
        shard_of[:, :, None] == jnp.arange(shards, dtype=jnp.int32)[None, None, :]
    ) & is_valid[:, :, None]
    rank_hit = rank_of[:, :, None] == jnp.arange(capacity, dtype=jnp.int32)[None, None, :]
    slot_hits = (shard_hit[:, :, :, None] & rank_hit[:, :, None, :]).astype(jnp.int32)
    slot_local = jnp.sum(slot_hits * local_of[:, :, None, None], axis=1)
    slot_live = jnp.sum(slot_hits, axis=1) > 0
    return (slot_local, slot_live)


def piece_rows(owned_slots, count_rows):
    row_index = jnp.arange(count_rows, dtype=jnp.int32)
    slot_index = row_index // BLOCK
    return jnp.take(owned_slots, slot_index, axis=1) * BLOCK + (row_index % BLOCK)[None, :]


def body(q_latent, index_query, index_weight, index_keys, latent_cache, block_ids, block_counts):
    shards = lax.axis_size("ctx")
    shard_here = lax.axis_index("ctx")
    keys_dev = latent_cache.shape[0]
    feature_width = latent_cache.shape[1]
    latent_width = feature_width - ROPE
    blocks_dev = keys_dev // BLOCK
    slot_local, slot_live = slot_tables(block_ids, block_counts, blocks_dev, shards, CAP)
    head_query = lax.all_to_all(q_latent, "head", split_axis=1, concat_axis=0, tiled=True)
    owned_slots = lax.dynamic_index_in_dim(slot_local, shard_here, axis=1, keepdims=False)
    span_rows = CAP * BLOCK
    row_ids = piece_rows(owned_slots, span_rows)
    outgoing = jnp.take(latent_cache, row_ids.reshape(-1), axis=0).reshape(
        shards, span_rows, feature_width
    )
    gathered = lax.all_to_all(outgoing, "ctx", split_axis=0, concat_axis=0, tiled=True)
    key_span = 8 * BLOCK
    query_rows = index_query.shape[0]

    def score_span(block_index, scores_sofar):
        key_block = lax.dynamic_slice_in_dim(index_keys, block_index * key_span, key_span, 0)
        block_scores = index_block(index_query, index_weight, key_block)
        return lax.dynamic_update_slice_in_dim(
            scores_sofar, block_scores, block_index * key_span, 1
        )

    index_scores = lax.fori_loop(
        0, keys_dev // key_span, score_span, jnp.zeros((query_rows, keys_dev), jnp.float32)
    )
    recv_local = lax.dynamic_index_in_dim(slot_local, shard_here, axis=0, keepdims=False)
    recv_live = lax.dynamic_index_in_dim(slot_live, shard_here, axis=0, keepdims=False)
    shard_base = jnp.arange(shards, dtype=jnp.int32)[:, None] * blocks_dev + recv_local
    key_pos = (
        shard_base[:, :, None] * BLOCK + jnp.arange(BLOCK, dtype=jnp.int32)[None, None, :]
    ).reshape(-1)
    key_live = jnp.broadcast_to(recv_live[:, :, None], recv_live.shape + (BLOCK,)).reshape(-1)
    query_pos = shards * (keys_dev - TILE) + shard_here * TILE + jnp.arange(TILE, dtype=jnp.int32)
    allowed = key_live[None, :] & (key_pos[None, :] <= query_pos[:, None])
    key_rows = gathered.reshape(-1, feature_width)
    attention = attend_rows(head_query, key_rows, allowed, latent_width)
    return (attention, index_scores)


def solution(mesh):
    return jax.shard_map(
        body,
        mesh=mesh,
        in_specs=(
            P(("ctx", "head"), None, None),
            P("head", None, None),
            P("head", None),
            P("ctx", None),
            P("ctx", None),
            P(),
            P(),
        ),
        out_specs=(P("ctx", "head", None), P("head", "ctx")),
        check_vma=False,
    )
```

profile of v0, /device:TPU:0, one launch (start us, length us, event | category | flops | bytes accessed | tf_op | source)
XLA Modules:
  0.0 184.5 jit_solution(5094813790023461558)
XLA Ops:
  3.1 1.0 gather_fusion
  4.5 3.1 %copy.43 = bf16[2048,576]{1,0:T(8,128)(2,1)S(1)} copy(bf16[2048,576]{0,1:T(8,128)(2,1)} %param.13) | data formatting | bytes 4718592 | tf_op args[4]
  7.6 9.3 %gather_fusion.1 = bf16[2048,576]{1,0:T(8,128)(2,1)} fusion(bf16[2048,576]{1,0:T(8,128)(2,1)S(1)} %copy.43, s32[2048]{0:T(1024)S(1)} %broadcast_clamp_fusion), kind=kCustom, calls=%fused_computation.1 | custom fusion | bytes 4726784 | tf_op jit(solution)/shard_map/jit(_take)/gather | solution.py:83
  16.9 2.9 %copy.44 = bf16[4,512,576]{1,2,0:T(8,128)(2,1)S(1)} copy(bf16[4,512,576]{2,1,0:T(8,128)(2,1)} %bitcast.61) | data formatting | bytes 4718592 | tf_op jit(solution)/shard_map/jit(_take)/gather | solution.py:83
  20.0 1.7 broadcast_select_fusion
  21.7 4.2 %all-to-all-start = ((bf16[4,512,576]{1,2,0:T(8,128)(2,1)}), bf16[4,512,576]{1,2,0:T(8,128)(2,1)S(1)}, u32[]{:S(2)}, u32[]{:S(2)}) async-start(bf16[4,512,576]{1,2,0:T(8,128)(2,1)} %broadcast_select_fusion), calls=%async_computation | async-start | bytes 4718592 | tf_op jit(solution)/shard_map/all_to_all | solution.py:86
  26.3 4.9 %copy.46 = bf16[16,128,576]{2,0,1:T(8,128)(2,1)} copy(bf16[16,128,576]{1,2,0:T(8,128)(2,1)} %param.9) | data formatting | bytes 4718592 | tf_op args[0]
  31.2 23.2 %all-to-all-done = bf16[4,512,576]{1,2,0:T(8,128)(2,1)S(1)} async-done(((bf16[4,512,576]{1,2,0:T(8,128)(2,1)}), bf16[4,512,576]{1,2,0:T(8,128)(2,1)S(1)}, u32[]{:S(2)}, u32[]{:S(2)}) %all-to-all-start) | async-done | bytes 2359328 | tf_op jit(solution)/shard_map/all_to_all | solution.py:86
  54.4 6.7 %all-to-all-start.1 = ((bf16[16,128,576]{2,0,1:T(8,128)(2,1)}), bf16[16,128,576]{2,0,1:T(8,128)(2,1)}, u32[]{:S(2)}, u32[]{:S(2)}) async-start(bf16[16,128,576]{2,0,1:T(8,128)(2,1)} %copy.46), calls=%async_computation.1 | async-start | bytes 5242880 | tf_op jit(solution)/shard_map/all_to_all | solution.py:79
  61.1 0.9 compare_and_fusion
  62.0 0.8 broadcast_in_dim.80
  62.8 76.1 %while.13 = (s32[]{:T(128)}, f32[64,2048]{1,0:T(8,128)}, bf16[2048,128]{1,0:T(8,128)(2,1)}, bf16[64,64,128]{2,1,0:T(8,128)(2,1)S(1)}, f32[64,64]{1,0:T(8,128)S(1...) while((s32[]{:T(128)}, f32[64,2048]{1,0:T(8,128)}, bf16[2048,128]{1,0:T(8,128)(2,1)}, ...), condition=%wide.region_7.8_spmd, body=%wide.region_5.7_spmd.sunk | while | flops 545226752 | bytes 35143828 | solution.py:97
  62.8 5.4 %maximum_bitcast_fusion.2 = f32[4096,512]{0,1:T(8,128)} fusion(bf16[4096,128]{1,0:T(8,128)(2,1)S(1)} %bitcast.58, bf16[2048,128]{1,0:T(8,128)(2,1)} %get-tuple-element.176, s32[]{:T(128)S(6)} %select_n.152), kind=kOutput, calls=%fused_computation.3.clone.1 | convolution fusion | flops 541065216 | bytes 9568260 | tf_op jit(solution)/shard_map/while/body/eval_jaxpr/dot_general | solution.py:17
  68.2 9.0 %copy.60 = f32[4096,512]{1,0:T(8,128)} copy(f32[4096,512]{0,1:T(8,128)} %maximum_bitcast_fusion.2) | data formatting | bytes 16777216 | tf_op jit(solution)/shard_map/while/body/eval_jaxpr/jit(relu)/max | solution.py:20
  77.2 4.0 %multiply_reduce_fusion.2 = f32[64,512]{1,0:T(8,128)S(1)} fusion(f32[64,64]{1,0:T(8,128)S(1)} %get-tuple-element.178, f32[4096,512]{1,0:T(8,128)} %copy.60), kind=kLoop, calls=%fused_computation.2.clone.1 | loop fusion | flops 4161536 | bytes 8536064 | tf_op jit(solution)/shard_map/while/body/eval_jaxpr/reduce_sum | solution.py:23
  81.9 5.4 %maximum_bitcast_fusion.2 = f32[4096,512]{0,1:T(8,128)} fusion(bf16[4096,128]{1,0:T(8,128)(2,1)S(1)} %bitcast.58, bf16[2048,128]{1,0:T(8,128)(2,1)} %get-tuple-element.176, s32[]{:T(128)S(6)} %select_n.152), kind=kOutput, calls=%fused_computation.3.clone.1 | convolution fusion | flops 541065216 | bytes 9568260 | tf_op jit(solution)/shard_map/while/body/eval_jaxpr/dot_general | solution.py:17
  87.3 9.0 %copy.60 = f32[4096,512]{1,0:T(8,128)} copy(f32[4096,512]{0,1:T(8,128)} %maximum_bitcast_fusion.2) | data formatting | bytes 16777216 | tf_op jit(solution)/shard_map/while/body/eval_jaxpr/jit(relu)/max | solution.py:20
  96.2 4.0 %multiply_reduce_fusion.2 = f32[64,512]{1,0:T(8,128)S(1)} fusion(f32[64,64]{1,0:T(8,128)S(1)} %get-tuple-element.178, f32[4096,512]{1,0:T(8,128)} %copy.60), kind=kLoop, calls=%fused_computation.2.clone.1 | loop fusion | flops 4161536 | bytes 8536064 | tf_op jit(solution)/shard_map/while/body/eval_jaxpr/reduce_sum | solution.py:23
  100.9 5.4 %maximum_bitcast_fusion.2 = f32[4096,512]{0,1:T(8,128)} fusion(bf16[4096,128]{1,0:T(8,128)(2,1)S(1)} %bitcast.58, bf16[2048,128]{1,0:T(8,128)(2,1)} %get-tuple-element.176, s32[]{:T(128)S(6)} %select_n.152), kind=kOutput, calls=%fused_computation.3.clone.1 | convolution fusion | flops 541065216 | bytes 9568260 | tf_op jit(solution)/shard_map/while/body/eval_jaxpr/dot_general | solution.py:17
  106.3 9.0 %copy.60 = f32[4096,512]{1,0:T(8,128)} copy(f32[4096,512]{0,1:T(8,128)} %maximum_bitcast_fusion.2) | data formatting | bytes 16777216 | tf_op jit(solution)/shard_map/while/body/eval_jaxpr/jit(relu)/max | solution.py:20
  115.3 4.0 %multiply_reduce_fusion.2 = f32[64,512]{1,0:T(8,128)S(1)} fusion(f32[64,64]{1,0:T(8,128)S(1)} %get-tuple-element.178, f32[4096,512]{1,0:T(8,128)} %copy.60), kind=kLoop, calls=%fused_computation.2.clone.1 | loop fusion | flops 4161536 | bytes 8536064 | tf_op jit(solution)/shard_map/while/body/eval_jaxpr/reduce_sum | solution.py:23
  119.9 5.4 %maximum_bitcast_fusion.2 = f32[4096,512]{0,1:T(8,128)} fusion(bf16[4096,128]{1,0:T(8,128)(2,1)S(1)} %bitcast.58, bf16[2048,128]{1,0:T(8,128)(2,1)} %get-tuple-element.176, s32[]{:T(128)S(6)} %select_n.152), kind=kOutput, calls=%fused_computation.3.clone.1 | convolution fusion | flops 541065216 | bytes 9568260 | tf_op jit(solution)/shard_map/while/body/eval_jaxpr/dot_general | solution.py:17
  125.3 9.0 %copy.60 = f32[4096,512]{1,0:T(8,128)} copy(f32[4096,512]{0,1:T(8,128)} %maximum_bitcast_fusion.2) | data formatting | bytes 16777216 | tf_op jit(solution)/shard_map/while/body/eval_jaxpr/jit(relu)/max | solution.py:20
  134.3 4.0 %multiply_reduce_fusion.2 = f32[64,512]{1,0:T(8,128)S(1)} fusion(f32[64,64]{1,0:T(8,128)S(1)} %get-tuple-element.178, f32[4096,512]{1,0:T(8,128)} %copy.60), kind=kLoop, calls=%fused_computation.2.clone.1 | loop fusion | flops 4161536 | bytes 8536064 | tf_op jit(solution)/shard_map/while/body/eval_jaxpr/reduce_sum | solution.py:23
  139.0 1.8 copy.53
  140.7 3.2 %copy.45 = bf16[4,512,576]{1,0,2:T(4,128)(2,1)} copy(bf16[4,512,576]{1,2,0:T(8,128)(2,1)S(1)} %all-to-all-done) | data formatting | bytes 4718592 | tf_op jit(solution)/shard_map/all_to_all | solution.py:86
  144.0 6.0 %reshape.328 = bf16[2048,576,1]{0,1,2:T(8,128)(2,1)} reshape(bf16[4,512,576]{1,0,2:T(4,128)(2,1)} %copy.45) | data formatting | bytes 4718592 | tf_op jit(solution)/shard_map/reshape | solution.py:109
  150.0 2.3 %copy.48 = bf16[8,16,16,576]{3,2,1,0:T(8,128)(2,1)S(1)} copy(bf16[8,16,16,576]{3,1,2,0:T(8,128)(2,1)} %bitcast.13) | data formatting | bytes 4718592 | tf_op jit(solution)/shard_map/all_to_all | solution.py:79
  152.3 8.2 %fusion.4 = (f32[2048]{0:T(1024)S(1)}, f32[2048,2048]{0,1:T(8,128)S(1)}) fusion(pred[128,2048]{1,0:T(8,128)(4,1)S(1)} %copy-done.2, bf16[2048,576]{1,0:T(8,128)(2,1)S(1)} %bitcast.60, bf16[2048,576]{0,1:T(8,128)(2,1)S(1)} %bitcast.62), kind=kOutput, calls=%fused_computation.11 | convolution fusion | flops 4844419072 | bytes 21766144 | tf_op jit(solution)/shard_map/dot_general | solution.py:30
  160.5 6.9 %fusion.3 = (bf16[2048,2048]{1,0:T(8,128)(2,1)}, f32[2048]{0:T(1024)S(1)}) fusion(f32[2048,2048]{0,1:T(8,128)S(1)} %get-tuple-element.124, f32[2048]{0:T(1024)S(1)} %get-tuple-element.123, pred[128,2048]{1,0:T(8,128)(4,1)S(1)} %copy-done.2), kind=kLoop, calls=%fused_computation.10 | loop fusion | flops 20969472 | bytes 25444352 | tf_op jit(solution)/shard_map/convert_element_type | solution.py:38
  167.5 14.4 %divide_convert_fusion = bf16[128,16,512]{2,0,1:T(8,128)(2,1)S(1)} fusion(f32[128,16]{0,1:T(8,128)S(1)} %copy.50, bf16[2048,576,1]{0,1,2:T(8,128)(2,1)S(1)} %copy-done.3, bf16[128,16,2048]{2,1,0:T(8,128)(2,1)} %bitcast.63), kind=kOutput, calls=%fused_computation.14 | convolution fusion | flops 4297064448 | bytes 12591104 | tf_op jit(solution)/shard_map/dot_general | solution.py:39
  182.0 2.5 %copy.51 = bf16[128,16,512]{2,1,0:T(8,128)(2,1)} copy(bf16[128,16,512]{2,0,1:T(8,128)(2,1)S(1)} %divide_convert_fusion) | data formatting | bytes 4194304
  (44 shorter events, 6.1 us)
Async XLA Ops:
  21.7 32.7 %all-to-all-start = ((bf16[4,512,576]{1,2,0:T(8,128)(2,1)}), bf16[4,512,576]{1,2,0:T(8,128)(2,1)S(1)}, u32[]{:S(2)}, u32[]{:S(2)}) async-start(bf16[4,512,576]{1,2,0:T(8,128)(2,1)} %broadcast_select_fusion), calls=%async_computation | async-start | bytes 4718592 | tf_op jit(solution)/shard_map/all_to_all | solution.py:86
  31.2 31.7 %copy-start = (bf16[64,64,128]{2,1,0:T(8,128)(2,1)S(1)}, bf16[64,64,128]{2,1,0:T(8,128)(2,1)}, u32[]{:S(2)}) copy-start(bf16[64,64,128]{2,1,0:T(8,128)(2,1)} %param.10) | copy-start | bytes 3145732
  31.2 31.7 %copy-start.4 = (f32[64,64]{1,0:T(8,128)S(1)}, f32[64,64]{1,0:T(8,128)}, u32[]{:S(2)}) copy-start(f32[64,64]{1,0:T(8,128)} %param.11) | copy-start | bytes 49156
  54.4 95.6 %all-to-all-start.1 = ((bf16[16,128,576]{2,0,1:T(8,128)(2,1)}), bf16[16,128,576]{2,0,1:T(8,128)(2,1)}, u32[]{:S(2)}, u32[]{:S(2)}) async-start(bf16[16,128,576]{2,0,1:T(8,128)(2,1)} %copy.46), calls=%async_computation.1 | async-start | bytes 5242880 | tf_op jit(solution)/shard_map/all_to_all | solution.py:79
  143.9 8.3 %copy-start.1 = (bf16[4,72,8,512]{3,2,0,1:T(8,128)(2,1)S(1)}, bf16[4,72,8,512]{3,2,0,1:T(8,128)(2,1)}, u32[]{:S(2)}) copy-start(bf16[4,72,8,512]{3,2,0,1:T(8,128)(2,1)} %copy.53) | copy-start | bytes 7077892
  144.0 8.3 %copy-start.2 = (pred[128,2048]{1,0:T(8,128)(4,1)S(1)}, pred[128,2048]{1,0:T(8,128)(4,1)}, u32[]{:S(2)}) copy-start(pred[128,2048]{1,0:T(8,128)(4,1)} %compare_and_fusion) | copy-start | bytes 786436
  160.5 7.0 %copy-start.3 = (bf16[2048,576,1]{0,1,2:T(8,128)(2,1)S(1)}, bf16[2048,576,1]{0,1,2:T(8,128)(2,1)}, u32[]{:S(2)}) copy-start(bf16[2048,576,1]{0,1,2:T(8,128)(2,1)} %reshape.328) | copy-start | bytes 7077892
where the time goes:
time: 186 us; the launch traced here: 184 us
  local copies, waits for them, and re-layouts  77.2 us (42%)
  matrix products  44.2 us (24%)
  other arithmetic  28.1 us (15%)
  waiting for transfers between devices  23.2 us (12%)
  starting transfers between devices  10.9 us (6%)
    max x4, local copies, waits for them, and re-layouts, index_block(): jax.nn.relu(raw_dots * index_query.shape[2] ** (-0.5))  35.9 us
    all_to_all x1, waiting for transfers between devices, body(): lax.all_to_all(outgoing, 'ctx', split_axis=0, concat_axis=0, tiled=True)  23.2 us
    dot_general x4, matrix products, index_block(): lax.dot_general(flat_query, key_block, (((1,), (1,)), ((), ())), preferre...  21.5 us
    reduce_sum x4, other arithmetic, index_block(): return jnp.sum(gated_dots * index_weight[:, :, None], axis=1)  15.9 us
    dot_general x1, matrix products, attend_rows(): full_sum = jnp.dot(weights, key_rows, preferred_element_type=jnp.float32)  14.4 us
    gather x2, local copies, waits for them, and re-layouts, body(): jnp.take(latent_cache, row_ids.reshape(-1), axis=0)  12.3 us
    unnamed x14, local copies, waits for them, and re-layouts  10.5 us
    dot_general x1, matrix products, attend_rows(): lax.dot_general(flat_query, key_rows, (((1,), (1,)), ((), ())), preferred...  8.2 us
  transfers between devices with their start and end apart: 2, of which 1 were waited for; matrix products, arithmetic and copies ran while one was open for 51% of the time, Pallas kernels for 0%

commit v1 on v0

v1 whole, which is shorter than its diff:
```python
import functools

import jax
import jax.numpy as jnp
from jax import lax
from jax.experimental import pallas as pl
from jax.experimental.pallas import tpu as pltpu
from jax.sharding import PartitionSpec as P

ROPE = 64
BLOCK = 64
CAP = 8
LANES = 128
FAR = 1 << 28

softmax_scale = 192.0 ** (-0.5)


def flip(index, mask, bits):
    total = 0
    for b in range(bits):
        w = 1 << b
        total = total + lax.rem(lax.div(index, w) + (mask // w) % 2, 2) * w
    return total


def kernel(
    C, H,
    q_hbm, iq_hbm, iw_hbm, ik_hbm, cache_hbm, ids, counts,
    att_hbm, idx_hbm,
    q_v, iq_v, iw_v, ik_v, cache_v, stage, recv, ksend, krecv, kpos, wcol, obuf, ibuf,
    in_sem, qs_sem, qr_sem, ks_sem, kr_sem, own_sem, out_sem, idx_sem,
):
    ctx = lax.axis_index("ctx")
    head = lax.axis_index("head")
    nq, heads, feat = q_v.shape
    lat = feat - ROPE
    hs = heads // H
    rows = nq * hs
    half = rows // 2
    lat_tiles = lat // LANES
    blocks_dev = cache_v.shape[0]
    keys_dev = blocks_dev * BLOCK
    nsel = ids.shape[1]
    tile = nq * H
    span = CAP * BLOCK
    keys = C * span
    bits = H.bit_length() - 1

    loads = [
        pltpu.make_async_copy(q_hbm, q_v, in_sem.at[0]),
        pltpu.make_async_copy(cache_hbm, cache_v, in_sem.at[1]),
        pltpu.make_async_copy(iw_hbm, iw_v, in_sem.at[2]),
        pltpu.make_async_copy(iq_hbm, iq_v, in_sem.at[3]),
        pltpu.make_async_copy(ik_hbm, ik_v, in_sem.at[4]),
    ]
    for copy in loads:
        copy.start()

    barrier = pltpu.get_barrier_semaphore()
    for k in range(1, H):
        pl.semaphore_signal(barrier, inc=1, device_id={"head": flip(head, k, bits)},
                            device_id_type=pl.DeviceIdType.MESH)
    for k in range(1, C):
        pl.semaphore_signal(barrier, inc=1, device_id={"ctx": lax.rem(ctx + k, C)},
                            device_id_type=pl.DeviceIdType.MESH)

    loads[0].wait()
    for p in range(H):
        piece = q_v[:, p * hs:(p + 1) * hs, :].astype(jnp.float32).reshape(rows, feat)
        for t in range(lat_tiles):
            stage[p, t * rows:(t + 1) * rows, :] = piece[:, t * LANES:(t + 1) * LANES].astype(jnp.bfloat16)
        rope = piece[:, lat:]
        stage[p, lat_tiles * rows:, :] = jnp.concatenate([rope[:half], rope[half:]], axis=1).astype(jnp.bfloat16)

    pl.semaphore_wait(barrier, H - 1 + C - 1)

    order = list(range(H - 1, 0, -1))

    def q_copy(k):
        peer = flip(head, k, bits)
        return pltpu.make_async_remote_copy(
            src_ref=stage.at[peer], dst_ref=recv.at[head],
            send_sem=qs_sem.at[k - 1], recv_sem=qr_sem.at[k - 1],
            device_id={"head": peer}, device_id_type=pl.DeviceIdType.MESH)

    for k in order:
        q_copy(k).start()

    def slots(tile_index, shard):
        count = counts[tile_index]

        n = jnp.int32(0)
        table = [jnp.int32(-1)] * CAP
        for e in range(nsel):
            block = ids[tile_index, e]
            mine = jnp.logical_and(e < count, lax.div(block, blocks_dev) == shard)
            local = lax.rem(block, blocks_dev)
            table = [
                jnp.where(jnp.logical_and(mine, n == s), local, old) for s, old in enumerate(table)
            ]
            n = n + mine.astype(jnp.int32)
        return table

    loads[1].wait()

    def k_copy(d):
        to = lax.rem(ctx + d, C)
        return pltpu.make_async_remote_copy(
            src_ref=ksend.at[to], dst_ref=krecv.at[ctx],
            send_sem=ks_sem.at[d - 1], recv_sem=kr_sem.at[d - 1],
            device_id={"ctx": to}, device_id_type=pl.DeviceIdType.MESH)

    pad = jnp.zeros((BLOCK, LANES - ROPE), jnp.bfloat16)
    near = [d for d in range(1, C)]
    for d in near + [0]:
        to = lax.rem(ctx + d, C)
        for s, local in enumerate(slots(to, ctx)):
            part = cache_v[jnp.maximum(local, 0)]
            ksend[to, s * BLOCK:(s + 1) * BLOCK, :lat] = part[:, :lat]
            ksend[to, s * BLOCK:(s + 1) * BLOCK, lat:] = jnp.concatenate([part[:, lat:], pad], axis=1)
        if d:
            k_copy(d).start()
    own = pltpu.make_async_copy(ksend.at[ctx], krecv.at[ctx], own_sem)
    own.start()

    lane = lax.broadcasted_iota(jnp.int32, (1, LANES), 1)
    per = LANES // BLOCK
    for shard in range(C):
        table = slots(ctx, jnp.int32(shard))
        bases = [
            jnp.where(local < 0, FAR, (shard * blocks_dev + local) * BLOCK) for local in table
        ]
        for j in range(CAP // per):
            low, high = bases[j * per], bases[j * per + 1]
            kpos[0:1, shard * span + j * LANES:shard * span + (j + 1) * LANES] = jnp.where(
                lane < BLOCK, low + lane, high + (lane - BLOCK))

    iqn, ih, idim = iq_hbm.shape
    for n in (2, 3, 4):
        loads[n].wait()
    w_t = (iw_v[...] * (idim ** -0.5)).T
    for i in range(iqn):
        wcol[i] = jnp.broadcast_to(w_t[:, i:i + 1], (ih, LANES))
    group = 8
    wide = 256

    def index_step(g, _):
        qs = iq_v[pl.ds(g * group, group)].reshape(group * ih, idim)
        w = wcol[pl.ds(g * group, group)]
        for j in range(keys_dev // wide):
            dots = lax.dot_general(
                qs, ik_v[j * wide:(j + 1) * wide, :], (((1,), (1,)), ((), ())),
                preferred_element_type=jnp.float32)
            gated = jnp.maximum(dots, 0.0).reshape(group, ih, wide)
            for u in range(wide // LANES):
                ibuf[pl.ds(pl.multiple_of(g * group, group), group), j * wide + u * LANES:j * wide + (u + 1) * LANES] = jnp.sum(
                    gated[:, :, u * LANES:(u + 1) * LANES] * w, axis=1)
        return 0

    lax.fori_loop(0, iqn // group, index_step, 0)
    idx_out = pltpu.make_async_copy(ibuf, idx_hbm, idx_sem)
    idx_out.start()

    own.wait()
    for d in near:
        k_copy(d).wait_send()
        source = lax.rem(ctx - d + C, C)
        pltpu.make_async_remote_copy(
            src_ref=ksend.at[source], dst_ref=krecv.at[source],
            send_sem=ks_sem.at[d - 1], recv_sem=kr_sem.at[d - 1],
            device_id={"ctx": source}, device_id_type=pl.DeviceIdType.MESH).wait_recv()

    def attend(chunk_ref, source):
        parts = [chunk_ref[t * rows:(t + 1) * rows, :] for t in range(lat_tiles)]
        pair = chunk_ref[lat_tiles * rows:, :].astype(jnp.float32)
        turned = jnp.concatenate([pair[:, ROPE:], pair[:, :ROPE]], axis=1)
        rope = jnp.concatenate([pair, turned], axis=0).astype(jnp.bfloat16)
        lhs = jnp.concatenate(parts + [rope], axis=1)
        key_rows = krecv[...].reshape(keys, lat + LANES)
        scores = lax.dot_general(
            lhs, key_rows, (((1,), (1,)), ((), ())), preferred_element_type=jnp.float32
        ) * softmax_scale
        first = C * (keys_dev - tile) + ctx * tile + source * nq
        qpos = first + lax.broadcasted_iota(jnp.int32, (rows, 1), 0) // hs
        scores = jnp.where(kpos[...] <= qpos, scores, -jnp.inf)
        top = jnp.max(scores, axis=1, keepdims=True)
        expd = jnp.exp(scores - top)
        total = jnp.sum(expd, axis=1, keepdims=True)
        out = jnp.dot(expd.astype(jnp.bfloat16), key_rows[:, :lat], preferred_element_type=jnp.float32)
        out = out * (1.0 / total)
        obuf[source] = out.reshape(nq, hs, lat).astype(jnp.bfloat16)

    def out_copy(source):
        return pltpu.make_async_copy(
            obuf.at[source], att_hbm.at[pl.ds(source * nq, nq)], out_sem.at[source])

    attend(stage.at[head], head)
    out_copy(head).start()

    def peer_step(i, _):
        k = H - 1 - i
        peer = flip(head, k, bits)
        pltpu.make_async_remote_copy(
            src_ref=stage.at[peer], dst_ref=recv.at[peer],
            send_sem=qs_sem.at[k - 1], recv_sem=qr_sem.at[k - 1],
            device_id={"head": peer}, device_id_type=pl.DeviceIdType.MESH).wait()
        attend(recv.at[peer], peer)
        out_copy(peer).start()
        return 0

    lax.fori_loop(0, H - 1, peer_step, 0)
    for source in range(H):
        out_copy(source).wait()
    idx_out.wait()


def body(q_latent, index_query, index_weight, index_keys, latent_cache, block_ids, block_counts):
    C = lax.axis_size("ctx")
    H = lax.axis_size("head")
    nq, heads, feat = q_latent.shape
    lat = feat - ROPE
    hs = heads // H
    rows = nq * hs
    keys_dev = latent_cache.shape[0]
    span = CAP * BLOCK
    packed = rows * (lat // LANES) + rows // 2
    iqn, ih, idim = index_query.shape
    any_spec = pl.BlockSpec(memory_space=pl.ANY)
    smem = pl.BlockSpec(memory_space=pltpu.SMEM)
    bf16, f32 = jnp.bfloat16, jnp.float32
    dma = pltpu.SemaphoreType.DMA
    return pl.pallas_call(
        functools.partial(kernel, C, H),
        out_shape=(
            jax.ShapeDtypeStruct((nq * H, hs, lat), bf16),
            jax.ShapeDtypeStruct((iqn, keys_dev), f32),
        ),
        in_specs=[any_spec] * 5 + [smem] * 2,
        out_specs=(any_spec, any_spec),
        scratch_shapes=[
            pltpu.VMEM((nq, heads, feat), bf16),
            pltpu.VMEM((iqn, ih, idim), bf16),
            pltpu.VMEM((iqn, ih), f32),
            pltpu.VMEM((keys_dev, idim), bf16),
            pltpu.VMEM((keys_dev // BLOCK, BLOCK, feat), bf16),
            pltpu.VMEM((H, packed, LANES), bf16),
            pltpu.VMEM((H, packed, LANES), bf16),
            pltpu.VMEM((C, span, lat + LANES), bf16),
            pltpu.VMEM((C, span, lat + LANES), bf16),
            pltpu.VMEM((1, C * span), jnp.int32),
            pltpu.VMEM((iqn, ih, LANES), f32),
            pltpu.VMEM((H, nq, hs, lat), bf16),
            pltpu.VMEM((iqn, keys_dev), f32),
            dma((5,)),
            dma((H - 1,)),
            dma((H - 1,)),
            dma((C - 1,)),
            dma((C - 1,)),
            dma(()),
            dma((H,)),
            dma(()),
        ],
        compiler_params=pltpu.CompilerParams(
            collective_id=0, has_side_effects=True, vmem_limit_bytes=56 * 1024 * 1024
        ),
        cost_estimate=pl.CostEstimate(flops=12_000_000_000, bytes_accessed=12_000_000, transcendentals=4_000_000),
    )(q_latent, index_query, index_weight, index_keys, latent_cache.reshape(keys_dev // BLOCK, BLOCK, feat),
      block_ids, block_counts)


def solution(mesh):
    return jax.shard_map(
        body,
        mesh=mesh,
        in_specs=(
            P(("ctx", "head"), None, None),
            P("head", None, None),
            P("head", None),
            P("ctx", None),
            P("ctx", None),
            P(),
            P(),
        ),
        out_specs=(P("ctx", "head", None), P("head", "ctx")),
        check_vma=False,
    )
```

time: 186 us -> 81.9 us (0.44)
  Pallas kernels: 0 us -> 70 us
  local copies, waits for them, and re-layouts: 77.2 us -> 11 us
  matrix products: 44.2 us -> 0 us
  other arithmetic: 28.1 us -> 0 us
  waiting for transfers between devices: 23.2 us -> 0 us
  starting transfers between devices: 10.9 us -> 0 us
    pallas_call x0 -> x1, Pallas kernels: none -> 70 us  [body(): pl.pallas_call(functools.partial(kernel, C, H), out_shape=(jax.ShapeDtype...]
    dot_general x6 -> x0, matrix products: 44.2 us -> none  [the longest x4 21.5 us: index_block(): lax.dot_general(flat_query, key_block, (((1,), (1,)), ((), ())), preferre...]
    max x4 -> x0, local copies, waits for them, and re-layouts: 35.9 us -> none  [index_block(): jax.nn.relu(raw_dots * index_query.shape[2] ** (-0.5))]
    all_to_all x2 -> x0, waiting for transfers between devices: 23.2 us -> none  [the longest x1 23.2 us: body(): lax.all_to_all(outgoing, 'ctx', split_axis=0, concat_axis=0, tiled=True)]
    reduce_sum x6 -> x0, other arithmetic: 16.8 us -> none  [the longest x4 15.9 us: index_block(): return jnp.sum(gated_dots * index_weight[:, :, None], axis=1)]
    gather x3 -> x0, local copies, waits for them, and re-layouts: 13.3 us -> none  [the longest x2 12.3 us: body(): jnp.take(latent_cache, row_ids.reshape(-1), axis=0)]
    all_to_all x2 -> x0, starting transfers between devices: 10.9 us -> none  [the longest x1 6.68 us: body(): lax.all_to_all(q_latent, 'head', split_axis=1, concat_axis=0, tiled=True)]
    reshape x2 -> x0, local copies, waits for them, and re-layouts: 7.79 us -> none  [body(): key_rows = gathered.reshape(-1, feature_width)]
  transfers between devices with their start and end apart: 2 -> 0, of which waited for: 1 -> 0; matrix products, arithmetic and copies ran while one was open for 51% -> 0% of each run, Pallas kernels for 0% -> 0%
where the time goes in v1:
time: 81.9 us; the launch traced here: 81.7 us
  Pallas kernels  70 us (85%)
  local copies, waits for them, and re-layouts  11 us (13%)
    pallas_call x1, Pallas kernels, body(): pl.pallas_call(functools.partial(kernel, C, H), out_shape=(jax.ShapeDtype...  70 us
    unnamed x8, local copies, waits for them, and re-layouts  11 us

profile of v1, /device:TPU:0, one launch (start us, length us, event | category | flops | bytes accessed | tf_op | source)
XLA Modules:
  0.0 81.7 jit_solution(15213141705160251454)
XLA Ops:
  0.6 0.0 copy-start
  0.6 4.5 %copy.10.q_hbm = bf16[16,128,576]{2,1,0:T(8,128)(2,1)} copy(bf16[16,128,576]{1,2,0:T(8,128)(2,1)} %param.7) | data formatting | bytes 4718592 | tf_op args[0]
  5.1 0.0 copy-done
  5.1 2.6 %copy.9 = bf16[2048,576]{1,0:T(8,128)(2,1)} copy(bf16[2048,576]{0,1:T(8,128)(2,1)S(1)} %copy-done) | data formatting | bytes 4718592 | tf_op args[4]
  7.7 70.0 %shard_map.86 = (bf16[128,16,512]{2,1,0:T(8,128)(2,1)}, f32[64,2048]{1,0:T(8,128)}) custom-call(bf16[16,128,576]{2,1,0:T(8,128)(2,1)} %copy.10.q_hbm, bf16[64,64,128]{2,1,0:T(8,128)(2,1)} %iq_hbm.1, f32[64,64]{1,0:T(8,128)} %iw_hbm.1, bf16[2048,128]{1,0:T(8,128)(2,1)} %ik_hbm.1, bf16[32,64,576]{2,1,0:T(8,128)(2,1)} %bitcast.1, s32[4,32]{1,0:T(4,128)} %ids.1, ...), custom_call_target="tpu_custom_call" | custom-call | flops 12000000000 | bytes 12000000 | tf_op jit(solution)/shard_map/pallas_call | solution.py:233
  77.8 0.0 copy-start.1
  77.8 3.1 %copy.13 = bf16[128,16,512]{2,1,0:T(8,128)(2,1)} copy(bf16[128,16,512]{2,1,0:T(8,128)(2,1)} %get-tuple-element.4) | data formatting | bytes 4194304
  80.9 0.0 copy-done.1
  80.9 0.8 copy.14
Async XLA Ops:
  0.6 4.5 %copy-start = (bf16[2048,576]{0,1:T(8,128)(2,1)S(1)}, bf16[2048,576]{0,1:T(8,128)(2,1)}, u32[]{:S(2)}) copy-start(bf16[2048,576]{0,1:T(8,128)(2,1)} %param.11) | copy-start | bytes 7077892
  77.8 3.1 %copy-start.1 = (f32[64,2048]{1,0:T(8,128)S(1)}, f32[64,2048]{1,0:T(8,128)}, u32[]{:S(2)}) copy-start(f32[64,2048]{1,0:T(8,128)} %get-tuple-element.5) | copy-start | bytes 1572868
